TPU v7x, 32 devices: a whole 2x2x4 slice. The times are simulated.
32 devices in a mesh: dp: 4 (over y, core), row: 8 (over z, x).
Axes of the slice: x: 2, y: 2, z: 4, core: 2. Of those that a mesh axis runs over, the one named last changes fastest.
Arguments:
- features: bfloat16 [4, 32, 256, 768], P('dp', 'row'), may hold values from -6 to 6
- cotangent: bfloat16 [4, 32, 256, 384], P('dp', 'row'), may hold values from -6 to 6
- projections: bfloat16 [3, 768, 384], P(None, 'dp'), may hold values from -0.21875 to 0.21875
- depths: int32 [4], replicated, may hold values from 1 to 32, as said below
Outputs:
- attended: bfloat16 [4, 32, 256, 384], P('dp', 'row')
- input_gradient: bfloat16 [4, 32, 256, 768], P('dp', 'row')
Inputs may be any that keep to these rules, and one draw needn't show every extreme that they name: `depths`: one MSA has depth 32 and another depth 1.
All inputs are finite; a program needn't handle non-finite values.
Results may differ from a plain program's by a relative error of at most 0.006.
The roundings to bfloat16 on the way count: a program that leaves them out, or rounds other values in their place, can miss the bound.
Values may be sent and summed in bfloat16 or wider, within the bound.
A program may use at most 64 MiB of HBM per device.

v0:
```python
import jax
import jax.numpy as jnp
from jax import lax
from jax.sharding import PartitionSpec as P

HEADS = 6


def softmax_rows(total, scale):
    logits = total * scale
    top = jnp.max(logits, axis=-1, keepdims=True)
    expo = jnp.exp(logits - top)
    return expo / jnp.sum(expo, axis=-1, keepdims=True)


def logit_grads(probs, dprobs, scale):
    inner = jnp.sum(probs * dprobs, axis=-1, keepdims=True)
    return (probs * (dprobs - inner) * scale).astype(jnp.bfloat16)


def local(features, cotangent, projections, depths):
    slots = features.shape[1]
    cols = features.shape[2]
    width = features.shape[3]
    inner_width = projections.shape[2]
    head_dim = inner_width // HEADS
    depth = lax.dynamic_index_in_dim(depths, lax.axis_index("dp"), keepdims=False)
    first_alignment = lax.axis_index("row") * slots
    live = (first_alignment + jnp.arange(slots, dtype=jnp.int32) < depth).astype(jnp.float32)
    scale = 1.0 / jnp.sqrt(jnp.float32(head_dim) * depth.astype(jnp.float32))
    flat = features.reshape(slots * cols, width)
    projected = jnp.einsum(
        "nc,pce->pne",
        flat,
        lax.all_gather(projections, "dp", axis=1, tiled=True),
        preferred_element_type=jnp.float32,
    ).astype(jnp.bfloat16)
    shaped = (slots, cols, HEADS, head_dim)
    queries = projected[0].reshape(shaped)
    keys = projected[1].reshape(shaped)
    values = projected[2].reshape(shaped)
    mask = live.astype(jnp.bfloat16)[:, None, None, None]
    masked_queries = queries * mask
    masked_grads = cotangent[0].reshape(shaped) * mask
    partial_logits = jnp.einsum(
        "rihd,rjhd->hij", masked_queries, keys, preferred_element_type=jnp.float32
    )
    partial_grads = jnp.einsum(
        "rihd,rjhd->hij", masked_grads, values, preferred_element_type=jnp.float32
    )
    logit_sum, grad_sum = lax.psum((partial_logits, partial_grads), "row")
    probs = softmax_rows(logit_sum, scale)
    probs_b = probs.astype(jnp.bfloat16)
    dlogits = logit_grads(probs, grad_sum, scale)
    attended = jnp.einsum("hij,rjhd->rihd", probs_b, values, preferred_element_type=jnp.float32)
    attended = (
        (attended * live[:, None, None, None])
        .astype(jnp.bfloat16)
        .reshape(1, slots, cols, inner_width)
    )
    dvalues = jnp.einsum(
        "hij,rihd->rjhd", probs_b, masked_grads, preferred_element_type=jnp.float32
    ).astype(jnp.bfloat16)
    dqueries = jnp.einsum(
        "hij,rjhd->rihd", dlogits, keys, preferred_element_type=jnp.float32
    ).astype(jnp.bfloat16)
    dkeys = jnp.einsum(
        "hij,rihd->rjhd", dlogits, masked_queries, preferred_element_type=jnp.float32
    ).astype(jnp.bfloat16)
    stacked = jnp.stack([dqueries, dkeys, dvalues]).reshape(3, slots * cols, inner_width)
    total = jnp.einsum(
        "pne,pce->nc",
        stacked,
        lax.all_gather(projections, "dp", axis=1, tiled=True),
        preferred_element_type=jnp.float32,
    )
    input_gradient = (total.reshape(slots, cols, width) * live[:, None, None]).astype(jnp.bfloat16)
    return (attended, input_gradient.reshape(1, slots, cols, width))


def solution(mesh):
    return jax.shard_map(
        local,
        mesh=mesh,
        in_specs=(P("dp", "row", None, None), P("dp", "row", None, None), P(None, "dp", None), P()),
        out_specs=(P("dp", "row", None, None), P("dp", "row", None, None)),
        check_vma=False,
    )
```

profile of v0, /device:TPU:0, one launch (start us, length us, event | category | flops | bytes accessed | tf_op | source)
XLA Modules:
  0.0 251.4 jit_solution(1027742943201666316)
XLA Ops:
  7.2 0.0 copy-start
  7.2 0.0 copy-start.8
  7.2 0.0 all-gather.2.cloned.1.call-start
  7.2 0.7 all-gather.2.cloned.1.call-update
  7.9 0.0 all-reduce.3.cloned.1.call-start
  8.0 2.3 copy.17
  10.3 0.0 copy-done.8
  10.3 0.7 dynamic_slice.4
  10.9 0.7 fusion.47
  11.6 21.5 %all-gather.2.cloned.1.call-done = bf16[3,768,384]{2,1,0:T(8,128)(2,1)} async-done(((bf16[3,192,384]{2,1,0:T(8,128)(2,1)}), bf16[3,768,384]{2,1,0:T(8,128)(2,1)}) %all-gather.2.cloned.1.call-update) | async-done | bytes 1769488 | tf_op jit(solution)/shard_map/all_gather | solution.py:35
  33.1 0.0 copy-done
  33.1 3.5 %convert_bitcast_fusion = bf16[3,1024,384]{1,2,0:T(8,128)(2,1)S(1)} fusion(bf16[3,768,384]{2,1,0:T(8,128)(2,1)} %all-gather.2.cloned.1.call-done, bf16[1024,768,1]{1,0,2:T(8,128)(2,1)S(1)} %bitcast.70), kind=kOutput, calls=%fused_computation.5 | convolution fusion | flops 1813118976 | bytes 5701632 | tf_op jit(solution)/shard_map/nc,pce->pne/dot_general | solution.py:32
  36.7 1.1 fusion.48
  37.7 2.6 %reshape_squeeze.14 = bf16[4,256,6,64]{1,0,3,2:T(4,128)(2,1)} reshape(bf16[1,1024,384]{1,2,0:T(8,128)(2,1)} %get-tuple-element.8) | data formatting | bytes 1572864 | tf_op jit(solution)/shard_map/reshape;squeeze | solution.py:40
  40.4 1.4 reshape_squeeze.12
  41.8 0.0 copy-start.3
  41.8 1.5 reshape_squeeze.13
  43.3 0.0 copy-done.3
  43.3 0.0 copy-start.1
  43.3 1.4 broadcast_multiply_fusion
  44.7 0.0 copy-start.4
  44.7 0.0 copy-start.6
  44.7 0.0 copy-done.1
  44.7 0.0 copy-start.2
  44.7 1.6 convolution_bitcast_fusion
  46.3 0.0 copy-done.4
  46.3 0.0 copy-done.6
  46.4 0.1 copy-done.2
  46.4 1.6 convolution_bitcast_fusion.1
  48.0 0.0 all-reduce.3.cloned.1.call-update
  48.8 128.9 %all-reduce.3.cloned.1.call-done = (f32[6,256,256]{2,1,0:T(8,128)}, f32[6,256,256]{2,1,0:T(8,128)}) async-done(((f32[6,256,256]{2,1,0:T(8,128)}, f32[6,256,256]{2,1,0:T(8,128)}), (f32[6,256,256]{2,1,0:T(8,128)}, f32[6,256,256]{2,1,0:T(8,128)})) %all-reduce.3.cloned.1.call-update) | async-done | bytes 3145744 | tf_op jit(solution)/shard_map/psum | solution.py:51
  177.7 2.9 %fusion.49 = (f32[6,256]{1,0:T(8,128)S(1)}, f32[6,256,256]{2,1,0:T(8,128)}) fusion(f32[6,256,256]{2,1,0:T(8,128)} %get-tuple-element.4, f32[]{:T(128)S(6)} %sqrt.3), kind=kOutput, calls=%fused_computation.47 | output fusion | flops 1179903 | bytes 3151876 | tf_op jit(solution)/shard_map/sub | solution.py:12
  180.6 0.0 copy-start.7
  180.6 12.1 %fusion.13 = bf16[4,256,6,64]{1,3,0,2:T(8,128)(2,1)} fusion(f32[6,256,256]{2,1,0:T(8,128)} %get-tuple-element.5, bf16[4,256,6,64]{1,0,3,2:T(4,128)(2,1)S(1)} %copy-done.2, f32[]{:T(128)S(6)} %sqrt.3, f32[6,256,256]{2,1,0:T(8,128)} %get-tuple-element.14, f32[6,256]{1,0:T(8,128)S(1)} %get-tuple-element.13), kind=kOutput, calls=%fused_computation.21 | convolution fusion | flops 204474112 | bytes 4724740 | tf_op jit(solution)/shard_map/hij,rjhd->rihd/dot_general | solution.py:64
  192.7 0.0 copy-done.7
  192.7 0.0 copy-start.5
  192.7 12.1 %fusion.14 = bf16[4,256,6,64]{1,3,0,2:T(8,128)(2,1)} fusion(f32[6,256,256]{2,1,0:T(8,128)} %get-tuple-element.5, bf16[4,256,6,64]{1,3,2,0:T(8,128)(2,1)S(1)} %copy-done.7, f32[]{:T(128)S(6)} %sqrt.3, f32[6,256,256]{2,1,0:T(8,128)} %get-tuple-element.14, f32[6,256]{1,0:T(8,128)S(1)} %get-tuple-element.13), kind=kOutput, calls=%fused_computation.22 | convolution fusion | flops 204474112 | bytes 4724740 | tf_op jit(solution)/shard_map/hij,rihd->rjhd/dot_general | solution.py:67
  204.8 0.0 copy-done.5
  204.8 5.1 %fusion.15 = bf16[4,256,6,64]{1,3,0,2:T(8,128)(2,1)} fusion(bf16[4,256,6,64]{1,3,2,0:T(8,128)(2,1)S(1)} %copy-done.5, f32[6,256]{1,0:T(8,128)S(1)} %get-tuple-element.13, f32[6,256,256]{2,1,0:T(8,128)} %get-tuple-element.4, f32[]{:T(128)S(6)} %sqrt.3), kind=kOutput, calls=%fused_computation.23 | convolution fusion | flops 203294464 | bytes 3151876 | tf_op jit(solution)/shard_map/hij,rihd->rjhd/dot_general | solution.py:61
  209.9 1.7 copy.23
  211.7 0.6 stack.13
  212.3 2.6 %copy.21 = bf16[4,256,6,64]{1,0,3,2:T(4,128)(2,1)} copy(bf16[4,256,6,64]{1,3,0,2:T(8,128)(2,1)} %fusion.13) | data formatting | bytes 1572864 | tf_op jit(solution)/shard_map/convert_element_type | solution.py:66
  214.9 2.0 stack.12
  216.9 5.4 %fusion.16 = bf16[4,256,6,64]{1,3,0,2:T(8,128)(2,1)} fusion(bf16[4,256,6,64]{1,0,3,2:T(4,128)(2,1)} %reshape_squeeze.12, f32[4]{0:T(128)S(1)} %get-tuple-element.7, f32[6,256]{1,0:T(8,128)S(1)} %get-tuple-element.13, f32[6,256,256]{2,1,0:T(8,128)} %get-tuple-element.4, f32[]{:T(128)S(6)} %sqrt.3), kind=kOutput, calls=%fused_computation.24 | convolution fusion | flops 203687680 | bytes 3151892 | tf_op jit(solution)/shard_map/hij,rjhd->rihd/dot_general | solution.py:55
  222.4 2.1 copy.16
  224.5 2.3 copy.28
  226.8 2.6 %copy.25 = bf16[4,256,6,64]{1,0,3,2:T(4,128)(2,1)} copy(bf16[4,256,6,64]{1,3,0,2:T(8,128)(2,1)} %fusion.15) | data formatting | bytes 1572864 | tf_op jit(solution)/shard_map/convert_element_type | solution.py:63
  229.4 2.6 %stack.14 = bf16[1,1024,384]{1,2,0:T(8,128)(2,1)} reshape(bf16[4,256,6,64]{1,0,3,2:T(4,128)(2,1)} %copy.25) | data formatting | bytes 1572864 | tf_op jit(solution)/shard_map/stack | solution.py:70
  231.9 2.8 %maximum_bitcast_fusion = bf16[1024,384,3]{0,1,2:T(8,128)(2,1)} fusion(bf16[1,1024,384]{1,2,0:T(8,128)(2,1)} %stack.14, bf16[1,1024,384]{1,2,0:T(8,128)(2,1)S(1)} %stack.13, bf16[1,1024,384]{1,2,0:T(8,128)(2,1)S(1)} %stack.12), kind=kLoop, calls=%fused_computation.4 | loop fusion | flops 2359296 | bytes 4718592 | tf_op jit(solution)/shard_map/pne,pce->nc/dot_general | solution.py:71
  234.7 4.3 %copy.26 = bf16[1024,384,3]{1,0,2:T(8,128)(2,1)} copy(bf16[1024,384,3]{0,1,2:T(8,128)(2,1)} %maximum_bitcast_fusion) | data formatting | bytes 4718592 | tf_op jit(solution)/shard_map/pne,pce->nc/dot_general | solution.py:71
  239.0 5.6 %fusion.9 = bf16[1,4,256,768]{3,2,1,0:T(8,128)(2,1)} fusion(f32[4]{0:T(128)S(1)} %get-tuple-element.7, bf16[4,256,384,3]{2,1,0,3:T(8,128)(2,1)} %bitcast.73, bf16[3,768,384]{2,1,0:T(8,128)(2,1)} %all-gather.2.cloned.1.call-done), kind=kOutput, calls=%fused_computation.13 | convolution fusion | flops 1813512192 | bytes 5701648 | tf_op jit(solution)/shard_map/pne,pce->nc/dot_general | solution.py:71
Async XLA Ops:
  7.2 26.0 %copy-start = (bf16[1,4,256,768]{3,2,1,0:T(8,128)(2,1)S(1)}, bf16[1,4,256,768]{3,2,1,0:T(8,128)(2,1)}, u32[]{:S(2)}) copy-start(bf16[1,4,256,768]{3,2,1,0:T(8,128)(2,1)} %param.4) | copy-start | bytes 4718596
  7.2 3.1 %copy-start.8 = (s32[4]{0:T(128)S(1)}, s32[4]{0:T(128)}, u32[]{:S(2)}) copy-start(s32[4]{0:T(128)} %param.7) | copy-start | bytes 52
  7.2 25.9 %all-gather.2.cloned.1.call-start = ((), (), s32[]{:S(2)}) async-start(), calls=%async_computation | async-start | bytes 2211840 | tf_op jit(solution)/shard_map/all_gather | solution.py:35
  7.9 169.7 %all-reduce.3.cloned.1.call-start = ((), (), s32[]{:S(2)}) async-start(), calls=%async_computation.1 | async-start | bytes 6291456 | tf_op jit(solution)/shard_map/psum | solution.py:51
  41.8 1.5 copy-start.3
  43.3 1.4 copy-start.1
  44.7 1.6 copy-start.4
  44.7 1.7 copy-start.6
  44.7 1.7 copy-start.2
  180.6 12.1 %copy-start.7 = (bf16[4,256,6,64]{1,3,2,0:T(8,128)(2,1)S(1)}, bf16[4,256,6,64]{1,3,2,0:T(8,128)(2,1)}, u32[]{:S(2)}) copy-start(bf16[4,256,6,64]{1,3,2,0:T(8,128)(2,1)} %copy-done.6) | copy-start | bytes 2359300
  192.7 12.1 %copy-start.5 = (bf16[4,256,6,64]{1,3,2,0:T(8,128)(2,1)S(1)}, bf16[4,256,6,64]{1,3,2,0:T(8,128)(2,1)}, u32[]{:S(2)}) copy-start(bf16[4,256,6,64]{1,3,2,0:T(8,128)(2,1)} %copy-done.4) | copy-start | bytes 2359300
Sparse Core Ops, SparseCore 0:
  9.6 23.4 all-gather.1
  48.2 129.4 all-reduce.2
where the time goes:
time: 252 us; the launch traced here: 251 us
  waiting for transfers between devices  151 us (60%)
  matrix products  47 us (19%)
  local copies, waits for them, and re-layouts  30.5 us (12%)
  between operations  14.9 us (6%)
  other arithmetic  7.78 us (3%)
    psum x1, waiting for transfers between devices, local(): logit_sum, grad_sum = lax.psum((partial_logits, partial_grads), 'row')  129 us
    all_gather x1, waiting for transfers between devices, local(): lax.all_gather(projections, 'dp', axis=1, tiled=True)  21.5 us
    dot_general x1, matrix products, local(): jnp.einsum('hij,rihd->rjhd', dlogits, masked_queries, preferred_element_t...  12.1 us
    dot_general x1, matrix products, local(): jnp.einsum('hij,rjhd->rihd', dlogits, keys, preferred_element_type=jnp.fl...  12.1 us
    dot_general x1, matrix products, local(): jnp.einsum('pne,pce->nc', stacked, lax.all_gather(projections, 'dp', axis...  5.55 us
    dot_general x1, matrix products, local(): jnp.einsum('hij,rjhd->rihd', probs_b, values, preferred_element_type=jnp....  5.43 us
    another operation x3, local copies, waits for them, and re-layouts, local(): jnp.stack([dqueries, dkeys, dvalues]).reshape(3, slots * cols, inner_width)  5.16 us
    dot_general x1, matrix products, local(): jnp.einsum('hij,rihd->rjhd', probs_b, masked_grads, preferred_element_typ...  5.14 us
  transfers between devices with their start and end apart: 2, of which 2 were waited for; matrix products, arithmetic and copies ran while one was open for 1% of the time, Pallas kernels for 0%

commit v1 on v0

v1 whole, which is shorter than its diff:
```python
import functools

import jax
import jax.numpy as jnp
from jax import lax
from jax.experimental import pallas as pl
from jax.experimental.pallas import tpu as pltpu
from jax.sharding import PartitionSpec as P

HEADS = 6
F32 = jnp.float32
BF16 = jnp.bfloat16
MESH = pl.DeviceIdType.MESH
LAST = (((1,), (1,)), ((), ()))
FIRST = (((0,), (0,)), ((), ()))


def nt(a, b):
    return lax.dot_general(a, b, LAST, preferred_element_type=F32)


def tn(a, b):
    return lax.dot_general(a, b, FIRST, preferred_element_type=F32)


def nn(a, b):
    return jnp.dot(a, b, preferred_element_type=F32)


def gather_copies(dp):
    bits = []
    b = dp // 2
    while b:
        bits.append(b)
        b //= 2
    pairs = []
    for k, b in enumerate(bits):
        masks = [0]
        for hi in bits[:k]:
            masks += [m | hi for m in masks]
        pairs += [(m, b) for m in masks]
    return bits, pairs


def flip(me, mask):
    b = 1
    out = me
    while b <= mask:
        if mask & b:
            out = out + b - 2 * b * (lax.div(me, b) % 2)
        b *= 2
    return out


def live_of(depth, slot):
    return (slot < depth).astype(F32)


def tied_kernel(
    dp, ring, sub, gsub,
    feats_hbm, cot_hbm, proj_hbm, depths,
    qc_out, kc_out, vc_out, gc_out, wg_out, pd_out,
    feats, cot, wg, qc, kc, vc, gc, part, recv, pd,
    load_sem, store_sem, w_send, w_recv, r_send, r_recv, g_send, g_recv,
):
    me = lax.axis_index("dp")
    row = lax.axis_index("row")
    slots, cols, _ = feats.shape
    inner = cot.shape[2]
    hd = inner // HEADS
    shard = proj_hbm.shape[1]
    rows = part.shape[0] // ring
    half = rows // 2
    piece = half // sub
    lines = ring // 2

    def row_at(pos):
        z0 = pos
        z1 = ring - 1 - pos
        low = (pos < lines).astype(jnp.int32)
        return low * (2 * z0) + (1 - low) * (2 * z1 + 1)

    z = row // 2
    x = row % 2
    pos = z + x * (ring - 1 - 2 * z)
    right = row_at((pos + 1) % ring)
    left = row_at((pos + ring - 1) % ring)

    def shard_at(idx):
        return wg.at[:, pl.ds(pl.multiple_of(idx * shard, shard), shard), :]

    loads = [
        pltpu.make_async_copy(proj_hbm, shard_at(me), load_sem.at[0]),
        pltpu.make_async_copy(feats_hbm.at[0], feats, load_sem.at[1]),
        pltpu.make_async_copy(cot_hbm.at[0], cot, load_sem.at[2]),
    ]
    for c in loads:
        c.start()

    bits, pairs = gather_copies(dp)
    barrier = pltpu.get_barrier_semaphore()
    for b in bits:
        pl.semaphore_signal(barrier, inc=1, device_id=(flip(me, b), row), device_id_type=MESH)
    for n in (left, right):
        pl.semaphore_signal(barrier, inc=1, device_id=(me, n), device_id_type=MESH)
    pl.semaphore_wait(barrier, len(bits) + 2)

    def weight_copy(m, b):
        i = pairs.index((m, b))
        src = shard_at(flip(me, m))
        return pltpu.make_async_remote_copy(
            src_ref=src, dst_ref=src, send_sem=w_send.at[i], recv_sem=w_recv.at[i],
            device_id=(flip(me, b), row), device_id_type=MESH,
        )

    loads[0].wait()
    for b in bits:
        weight_copy(0, b).start()
    for m, b in pairs:
        weight_copy(m, b).wait_recv()
        for lower in bits:
            if lower < b:
                weight_copy(m | b, lower).start()
    loads[1].wait()
    loads[2].wait()

    depth = depths[me]
    first = row * slots
    for r in range(0, slots, 2):
        live = [live_of(depth, first + r + k) for k in range(2)]
        for p, dest in enumerate((qc, kc, vc, gc)):
            if p < 3:
                vals = [nn(feats[r + k], wg[p]) for k in range(2)]
            else:
                vals = [cot[r + k].astype(F32) for k in range(2)]
            if p == 0 or p == 3:
                vals = [v * l for v, l in zip(vals, live)]
            vals = [v.astype(BF16) for v in vals]
            for h in range(HEADS):
                dest[h, :, r * hd:(r + 2) * hd] = jnp.concatenate(
                    [v[:, h * hd:(h + 1) * hd] for v in vals], axis=1
                )

    stores = [
        pltpu.make_async_copy(s, d, store_sem.at[i])
        for i, (s, d) in enumerate(
            ((qc, qc_out), (kc, kc_out), (vc, vc_out), (gc, gc_out), (wg, wg_out))
        )
    ]

    for h in range(HEADS):
        at = slice(h * cols, (h + 1) * cols)
        part[at, 0:cols] = nt(qc[h], kc[h])
        part[at, cols:2 * cols] = nt(gc[h], vc[h])

    def part_rows(chunk, d, u):
        start = pl.multiple_of(chunk * rows + (d * half + u * piece), 8)
        return pl.ds(start, piece)

    def ring_copy(s, d, u):
        chunk = (pos + ring - 1 - s) % ring if d == 0 else (pos + 1 + s) % ring
        if s == 0:
            src = part.at[part_rows(chunk, d, u)]
        else:
            src = recv.at[d, s - 1, u]
        return pltpu.make_async_remote_copy(
            src_ref=src, dst_ref=recv.at[d, s, u],
            send_sem=r_send.at[d, s, u], recv_sem=r_recv.at[d, s, u],
            device_id=(me, right if d == 0 else left), device_id_type=MESH,
        )

    for u in range(sub):
        for d in range(2):
            ring_copy(0, d, u).start()
    for c in stores:
        c.start()
    for s in range(ring - 2):
        for u in range(sub):
            for d in range(2):
                ring_copy(s, d, u).wait_recv()
                chunk = (pos + 2 * ring - 2 - s) % ring if d == 0 else (pos + 2 + s) % ring
                recv[d, s, u] = recv[d, s, u] + part[part_rows(chunk, d, u)]
                ring_copy(s + 1, d, u).start()

    norm = lax.broadcast_in_dim(depth.astype(F32) * float(hd), (8, 128), ())
    scale = (1.0 / jnp.sqrt(norm))[0:1, 0:1]
    lastst = ring - 2

    def finish(d, u):
        ring_copy(lastst, d, u).wait_recv()
        total = recv[d, lastst, u] + part[part_rows(pos, d, u)]
        logits = total[:, 0:cols] * scale
        dprobs = total[:, cols:2 * cols]
        top = jnp.max(logits, axis=-1, keepdims=True)
        expo = jnp.exp(logits - top)
        probs = expo / jnp.sum(expo, axis=-1, keepdims=True)
        mean = jnp.sum(probs * dprobs, axis=-1, keepdims=True)
        return probs.astype(BF16), (probs * (dprobs - mean) * scale).astype(BF16)

    grow = rows // gsub

    def pd_rows(chunk, g):
        return pl.ds(pl.multiple_of(chunk * rows + g * grow, 16), grow)

    def spread_copy(s, d, g):
        chunk = (pos + ring - s) % ring if d == 0 else (pos + s) % ring
        ref = pd.at[pd_rows(chunk, g)]
        return pltpu.make_async_remote_copy(
            src_ref=ref, dst_ref=ref,
            send_sem=g_send.at[d, s, g], recv_sem=g_recv.at[d, s, g],
            device_id=(me, right if d == 0 else left), device_id_type=MESH,
        )

    def hops(d):
        out = []
        for s in range(lines):
            for g in range(gsub):
                if s < lines - 1 or (d == 0 and g == 0) or (d == 1 and g == 1):
                    out.append((s, g))
        return out

    def put(d):
        done = [finish(d, u) for u in range(sub)]
        probs = jnp.concatenate([a for a, _ in done], axis=0)
        dlog = jnp.concatenate([b for _, b in done], axis=0)
        return probs, dlog

    if gsub == 2:
        for d in range(2):
            probs, dlog = put(d)
            pd[pd_rows(pos, d), 0:cols] = probs
            pd[pd_rows(pos, d), cols:2 * cols] = dlog
            for e in range(2):
                if (0, d) in hops(e):
                    spread_copy(0, e, d).start()
    else:
        a, b = put(0), put(1)
        pd[pd_rows(pos, 0), 0:cols] = jnp.concatenate([a[0], b[0]], axis=0)
        pd[pd_rows(pos, 0), cols:2 * cols] = jnp.concatenate([a[1], b[1]], axis=0)
        for e in range(2):
            if (0, 0) in hops(e):
                spread_copy(0, e, 0).start()

    for s in range(lines):
        for g in range(gsub):
            for e in range(2):
                if (s, g) in hops(e):
                    spread_copy(s, e, g).wait_recv()
                    if (s + 1, g) in hops(e):
                        spread_copy(s + 1, e, g).start()

    last_store = pltpu.make_async_copy(pd, pd_out, store_sem.at[5])
    last_store.start()
    for m, b in pairs:
        weight_copy(m, b).wait_send()
    for s in range(ring - 1):
        for u in range(sub):
            for d in range(2):
                ring_copy(s, d, u).wait_send()
    for e in range(2):
        for s, g in hops(e):
            spread_copy(s, e, g).wait_send()
    for c in stores:
        c.wait()
    last_store.wait()


def output_kernel(qc, kc, vc, gc, wg, pd, depths, att, grad, stacked):
    slots, cols, inner = att.shape[1:]
    hd = inner // HEADS
    depth = depths[lax.axis_index("dp")]
    first = lax.axis_index("row") * slots
    live = [live_of(depth, first + r) for r in range(slots)]
    for h in range(0, HEADS, 2):
        got = []
        for k in range(2):
            n = h + k
            at = slice(n * cols, (n + 1) * cols)
            probs = pd[at, 0:cols]
            dlog = pd[at, cols:2 * cols]
            got.append((
                nn(probs, vc[n]),
                nn(dlog, kc[n]).astype(BF16),
                tn(dlog, qc[n]).astype(BF16),
                tn(probs, gc[n]).astype(BF16),
            ))
        lanes = slice(h * hd, (h + 2) * hd)
        for r in range(slots):
            cut = slice(r * hd, (r + 1) * hd)
            both = [jnp.concatenate([g[i][:, cut] for g in got], axis=1) for i in range(4)]
            att[0, r, :, lanes] = (both[0] * live[r]).astype(BF16)
            for i in range(3):
                stacked[i, r, :, lanes] = both[i + 1]
    for r in range(slots):
        total = nt(stacked[0, r], wg[0]) + nt(stacked[1, r], wg[1]) + nt(stacked[2, r], wg[2])
        grad[0, r] = (total * live[r]).astype(BF16)


def local(dp, ring, features, cotangent, projections, depths):
    _, slots, cols, width = features.shape
    inner = projections.shape[2]
    wide = slots * (inner // HEADS)
    rows = HEADS * cols // ring
    half = rows // 2
    sub = 2 if half % 16 == 0 else 1
    gsub = 2 if rows % 32 == 0 else 1
    _, pairs = gather_copies(dp)
    vmem = pl.BlockSpec(memory_space=pltpu.VMEM)
    anyspace = pl.BlockSpec(memory_space=pl.ANY)
    smem = pl.BlockSpec(memory_space=pltpu.SMEM)
    byhead = jax.ShapeDtypeStruct((HEADS, cols, wide), BF16)
    weights = (3, width, inner)
    pairshape = (HEADS * cols, 2 * cols)
    lines = ring // 2
    dma = pltpu.SemaphoreType.DMA
    *shaped, wg, pd = pl.pallas_call(
        functools.partial(tied_kernel, dp, ring, sub, gsub),
        out_shape=(
            byhead, byhead, byhead, byhead,
            jax.ShapeDtypeStruct(weights, BF16),
            jax.ShapeDtypeStruct(pairshape, BF16),
        ),
        in_specs=[anyspace, anyspace, anyspace, smem],
        out_specs=[anyspace] * 6,
        scratch_shapes=[
            pltpu.VMEM((slots, cols, width), BF16),
            pltpu.VMEM((slots, cols, inner), BF16),
            pltpu.VMEM(weights, BF16),
            *[pltpu.VMEM((HEADS, cols, wide), BF16)] * 4,
            pltpu.VMEM(pairshape, F32),
            pltpu.VMEM((2, ring - 1, sub, half // sub, 2 * cols), F32),
            pltpu.VMEM(pairshape, BF16),
            dma((3,)),
            dma((6,)),
            dma((len(pairs),)),
            dma((len(pairs),)),
            dma((2, ring - 1, sub)),
            dma((2, ring - 1, sub)),
            dma((2, lines, gsub)),
            dma((2, lines, gsub)),
        ],
        compiler_params=pltpu.CompilerParams(
            collective_id=0, has_side_effects=True, vmem_limit_bytes=40 * 2**20
        ),
    )(features, cotangent, projections, depths)
    return pl.pallas_call(
        output_kernel,
        out_shape=(
            jax.ShapeDtypeStruct((1, slots, cols, inner), BF16),
            jax.ShapeDtypeStruct((1, slots, cols, width), BF16),
        ),
        in_specs=[vmem] * 6 + [smem],
        out_specs=[vmem] * 2,
        scratch_shapes=[pltpu.VMEM((3, slots, cols, inner), BF16)],
        compiler_params=pltpu.CompilerParams(vmem_limit_bytes=40 * 2**20),
    )(*shaped, wg, pd, depths)


def solution(mesh):
    return jax.shard_map(
        functools.partial(local, mesh.shape["dp"], mesh.shape["row"]),
        mesh=mesh,
        in_specs=(P("dp", "row", None, None), P("dp", "row", None, None), P(None, "dp", None), P()),
        out_specs=(P("dp", "row", None, None), P("dp", "row", None, None)),
        check_vma=False,
    )
```

time: 252 us -> 84.6 us (0.34)
  waiting for transfers between devices: 151 us -> 0 us
  Pallas kernels: 0 us -> 79.5 us
  matrix products: 47 us -> 0 us
  local copies, waits for them, and re-layouts: 30.5 us -> 4.2 us
  between operations: 14.9 us -> 0.65 us
  other arithmetic: 7.78 us -> 0 us
    psum x1 -> x0, waiting for transfers between devices: 129 us -> none  [local(): logit_sum, grad_sum = lax.psum((partial_logits, partial_grads), 'row')]
    pallas_call x0 -> x2, Pallas kernels: none -> 79.5 us  [the longest x1 73.3 us: local(): pl.pallas_call(functools.partial(tied_kernel, dp, ring, sub, gsub), out_s...]
    dot_general x8 -> x0, matrix products: 47 us -> none  [the longest x1 12.1 us: local(): jnp.einsum('hij,rihd->rjhd', dlogits, masked_queries, preferred_element_t...]
    all_gather x1 -> x0, waiting for transfers between devices: 21.5 us -> none  [local(): lax.all_gather(projections, 'dp', axis=1, tiled=True)]
    another operation x6 -> x0, local copies, waits for them, and re-layouts: 10.7 us -> none  [the longest x3 5.16 us: local(): jnp.stack([dqueries, dkeys, dvalues]).reshape(3, slots * cols, inner_width)]
    convert_element_type x4 -> x0, local copies, waits for them, and re-layouts: 9.08 us -> none  [the longest x1 2.62 us: local(): dqueries = jnp.einsum('hij,rjhd->rihd', dlogits, keys, preferred_element_...]
    dot_general x1 -> x0, local copies, waits for them, and re-layouts: 4.27 us -> none  [local(): jnp.einsum('pne,pce->nc', stacked, lax.all_gather(projections, 'dp', axis...]
    sub x1 -> x0, other arithmetic: 2.9 us -> none  [softmax_rows(): expo = jnp.exp(logits - top)]
  transfers between devices with their start and end apart: 2 -> 0, of which waited for: 2 -> 0; matrix products, arithmetic and copies ran while one was open for 1% -> 0% of each run, Pallas kernels for 0% -> 0%
where the time goes in v1:
time: 84.6 us; the launch traced here: 84.3 us
  Pallas kernels  79.5 us (94%)
  local copies, waits for them, and re-layouts  4.2 us (5%)
    pallas_call x1, Pallas kernels, local(): pl.pallas_call(functools.partial(tied_kernel, dp, ring, sub, gsub), out_s...  73.3 us
    pallas_call x1, Pallas kernels, local(): pl.pallas_call(output_kernel, out_shape=(jax.ShapeDtypeStruct((1, slots,...  6.17 us
    unnamed x8, local copies, waits for them, and re-layouts  4.2 us

profile of v1, /device:TPU:0, one launch (start us, length us, event | category | flops | bytes accessed | tf_op | source)
XLA Modules:
  0.0 84.3 jit_solution(16143927768249458451)
XLA Ops:
  0.6 0.0 copy-start
  0.6 1.4 %copy-done = bf16[1,4,256,768]{3,2,1,0:T(8,128)(2,1)S(1)} copy-done((bf16[1,4,256,768]{3,2,1,0:T(8,128)(2,1)S(1)}, bf16[1,4,256,768]{3,2,1,0:T(8,128)(2,1)}, u32[]{:S(2)}) %copy-start) | copy-done | bytes 1572888
  2.0 0.0 copy-start.1
  2.0 1.1 %copy-done.1 = bf16[1,4,256,384]{3,2,1,0:T(8,128)(2,1)S(1)} copy-done((bf16[1,4,256,384]{3,2,1,0:T(8,128)(2,1)S(1)}, bf16[1,4,256,384]{3,2,1,0:T(8,128)(2,1)}, u32[]{:S(2)}) %copy-start.1) | copy-done | bytes 786456
  3.2 0.0 copy-start.2
  3.2 1.0 %copy-done.2 = bf16[3,192,384]{2,1,0:T(8,128)(2,1)S(1)} copy-done((bf16[3,192,384]{2,1,0:T(8,128)(2,1)S(1)}, bf16[3,192,384]{2,1,0:T(8,128)(2,1)}, u32[]{:S(2)}) %copy-start.2) | copy-done | bytes 442392
  4.2 0.0 copy-start.3
  4.2 0.7 copy-done.3
  4.8 73.3 %shard_map.59 = (bf16[6,256,256]{2,1,0:T(8,128)(2,1)S(1)}, bf16[6,256,256]{2,1,0:T(8,128)(2,1)S(1)}, bf16[6,256,256]{2,1,0:T(8,128)(2,1)S(1)}, bf16[6,256,256]{2...) custom-call(bf16[1,4,256,768]{3,2,1,0:T(8,128)(2,1)S(1)} %copy-done, ...), custom_call_target="tpu_custom_call" | custom-call | tf_op jit(solution)/shard_map/pallas_call | solution.py:316
  78.2 6.2 %shard_map.60 = (bf16[1,4,256,384]{3,2,1,0:T(8,128)(2,1)}, bf16[1,4,256,768]{3,2,1,0:T(8,128)(2,1)}) custom-call(bf16[6,256,256]{2,1,0:T(8,128)(2,1)S(1)} %get-tuple-element.8.qc, bf16[6,256,256]{2,1,0:T(8,128)(2,1)S(1)} %get-tuple-element.9.kc, bf16[6,256,256]{2,1,0:T(8,128)(2,1)S(1)} %get-tuple-element.10.vc, ...), custom_call_target="tpu_custom_call" | custom-call | tf_op jit(solution)/shard_map/pallas_call | solution.py:346
Async XLA Ops:
  0.6 1.4 %copy-start = (bf16[1,4,256,768]{3,2,1,0:T(8,128)(2,1)S(1)}, bf16[1,4,256,768]{3,2,1,0:T(8,128)(2,1)}, u32[]{:S(2)}) copy-start(bf16[1,4,256,768]{3,2,1,0:T(8,128)(2,1)} %feats_hbm.1) | copy-start | bytes 4718596
  2.0 1.1 %copy-start.1 = (bf16[1,4,256,384]{3,2,1,0:T(8,128)(2,1)S(1)}, bf16[1,4,256,384]{3,2,1,0:T(8,128)(2,1)}, u32[]{:S(2)}) copy-start(bf16[1,4,256,384]{3,2,1,0:T(8,128)(2,1)} %cot_hbm.1) | copy-start | bytes 2359300
  3.2 1.0 %copy-start.2 = (bf16[3,192,384]{2,1,0:T(8,128)(2,1)S(1)}, bf16[3,192,384]{2,1,0:T(8,128)(2,1)}, u32[]{:S(2)}) copy-start(bf16[3,192,384]{2,1,0:T(8,128)(2,1)} %proj_hbm.1) | copy-start | bytes 1327108
  4.2 0.7 copy-start.3

commit v2 on v1

v2 whole, which is shorter than its diff:
```python
import functools

import jax
import jax.numpy as jnp
from jax import lax
from jax.experimental import pallas as pl
from jax.experimental.pallas import tpu as pltpu
from jax.sharding import PartitionSpec as P

HEADS = 6
F32 = jnp.float32
BF16 = jnp.bfloat16
MESH = pl.DeviceIdType.MESH
LAST = (((1,), (1,)), ((), ()))
FIRST = (((0,), (0,)), ((), ()))


def nt(a, b):
    return lax.dot_general(a, b, LAST, preferred_element_type=F32)


def tn(a, b):
    return lax.dot_general(a, b, FIRST, preferred_element_type=F32)


def nn(a, b):
    return jnp.dot(a, b, preferred_element_type=F32)


def gather_copies(dp):
    bits = []
    b = dp // 2
    while b:
        bits.append(b)
        b //= 2
    pairs = []
    for k, b in enumerate(bits):
        masks = [0]
        for hi in bits[:k]:
            masks += [m | hi for m in masks]
        pairs += [(m, b) for m in masks]
    return bits, pairs


def flip(me, mask):
    b = 1
    out = me
    while b <= mask:
        if mask & b:
            out = out + b - 2 * b * (lax.div(me, b) % 2)
        b *= 2
    return out


def live_of(depth, slot):
    return (slot < depth).astype(F32)


def tied_kernel(
    dp, ring, gsub,
    feats_hbm, cot_hbm, proj_hbm, depths,
    qc_out, kc_out, vc_out, gc_out, wg_out, pd_out,
    feats, cot, wg, qc, kc, vc, gc, part, recv, pd,
    load_sem, store_sem, w_send, w_recv, r_send, r_recv, g_send, g_recv, g_store,
):
    me = lax.axis_index("dp")
    row = lax.axis_index("row")
    slots, cols, _ = feats.shape
    inner = cot.shape[2]
    hd = inner // HEADS
    shard = proj_hbm.shape[1]
    rows = part.shape[1] // ring
    half = rows // 2
    lines = ring // 2

    def row_at(pos):
        z0 = pos
        z1 = ring - 1 - pos
        low = (pos < lines).astype(jnp.int32)
        return low * (2 * z0) + (1 - low) * (2 * z1 + 1)

    z = row // 2
    x = row % 2
    pos = z + x * (ring - 1 - 2 * z)
    right = row_at((pos + 1) % ring)
    left = row_at((pos + ring - 1) % ring)

    groups = (slice(2 * inner, 3 * inner), slice(0, 2 * inner))

    def shard_at(idx, lanes):
        return wg.at[pl.ds(pl.multiple_of(idx * shard, shard), shard), lanes]

    loads = [
        pltpu.make_async_copy(
            proj_hbm.at[p], shard_at(me, slice(p * inner, (p + 1) * inner)), load_sem.at[p]
        )
        for p in range(3)
    ]
    loads.append(pltpu.make_async_copy(feats_hbm.at[0], feats, load_sem.at[3]))
    loads.append(pltpu.make_async_copy(cot_hbm.at[0], cot, load_sem.at[4]))
    for c in (loads[2], loads[0], loads[1], loads[3], loads[4]):
        c.start()

    bits, pairs = gather_copies(dp)
    barrier = pltpu.get_barrier_semaphore()
    for b in bits:
        pl.semaphore_signal(barrier, inc=1, device_id=(flip(me, b), row), device_id_type=MESH)
    for n in (left, right):
        pl.semaphore_signal(barrier, inc=1, device_id=(me, n), device_id_type=MESH)
    pl.semaphore_wait(barrier, len(bits) + 2)

    def weight_copy(t, m, b):
        i = pairs.index((m, b))
        src = shard_at(flip(me, m), groups[t])
        return pltpu.make_async_remote_copy(
            src_ref=src, dst_ref=src, send_sem=w_send.at[t, i], recv_sem=w_recv.at[t, i],
            device_id=(flip(me, b), row), device_id_type=MESH,
        )

    def weights_from(t, b):
        for m, at in pairs:
            if at == b:
                weight_copy(t, m, b).wait_recv()
                for lower in bits:
                    if lower < b:
                        weight_copy(t, m | b, lower).start()

    loads[2].wait()
    for b in bits:
        weight_copy(0, 0, b).start()
    weights_from(0, bits[0])
    loads[0].wait()
    loads[1].wait()
    for b in bits:
        weight_copy(1, 0, b).start()
    for b in bits[1:]:
        weights_from(0, b)

    depth = depths[me]
    first = row * slots

    def by_head(dest, vals, r):
        vals = [v.astype(BF16) for v in vals]
        for h in range(HEADS):
            dest[h, :, r * hd:(r + 2) * hd] = jnp.concatenate(
                [v[:, h * hd:(h + 1) * hd] for v in vals], axis=1
            )

    def live_at(r):
        return [live_of(depth, first + r + k) for k in range(2)]

    loads[3].wait()
    loads[4].wait()
    for r in range(0, slots, 2):
        by_head(gc, [cot[r + k].astype(F32) * l for k, l in enumerate(live_at(r))], r)
        by_head(vc, [nn(feats[r + k], wg[:, groups[0]]) for k in range(2)], r)
    for h in range(HEADS):
        part[0, h * cols:(h + 1) * cols, :] = nt(gc[h], vc[h])

    def part_rows(chunk, d):
        return pl.ds(pl.multiple_of(chunk * rows + d * half, 8), half)

    def ring_copy(s, d, u):
        chunk = (pos + ring - 1 - s) % ring if d == 0 else (pos + 1 + s) % ring
        if s == 0:
            src = part.at[u, part_rows(chunk, d)]
        else:
            src = recv.at[d, s - 1, u]
        return pltpu.make_async_remote_copy(
            src_ref=src, dst_ref=recv.at[d, s, u],
            send_sem=r_send.at[d, s, u], recv_sem=r_recv.at[d, s, u],
            device_id=(me, right if d == 0 else left), device_id_type=MESH,
        )

    def hop(s, u):
        for d in range(2):
            ring_copy(s, d, u).wait_recv()
            chunk = (pos + 2 * ring - 2 - s) % ring if d == 0 else (pos + 2 + s) % ring
            recv[d, s, u] = recv[d, s, u] + part[u, part_rows(chunk, d)]
            ring_copy(s + 1, d, u).start()

    for d in range(2):
        ring_copy(0, d, 0).start()
    weights_from(1, bits[0])
    hop(0, 0)
    for b in bits[1:]:
        weights_from(1, b)
    for r in range(0, slots, 2):
        both = [nn(feats[r + k], wg[:, groups[1]]) for k in range(2)]
        by_head(qc, [v[:, :inner] * l for v, l in zip(both, live_at(r))], r)
        by_head(kc, [v[:, inner:] for v in both], r)
        if r == 0:
            hop(1, 0)
    for h in range(HEADS):
        part[1, h * cols:(h + 1) * cols, :] = nt(qc[h], kc[h])
    for d in range(2):
        ring_copy(0, d, 1).start()

    stores = [
        pltpu.make_async_copy(s, d, store_sem.at[i])
        for i, (s, d) in enumerate(
            ((qc, qc_out), (kc, kc_out), (vc, vc_out), (gc, gc_out), (wg, wg_out))
        )
    ]
    for c in stores:
        c.start()
    for s in range(ring - 2):
        if s + 2 < ring - 2:
            hop(s + 2, 0)
        hop(s, 1)

    norm = lax.broadcast_in_dim(depth.astype(F32) * float(hd), (8, 128), ())
    scale = (1.0 / jnp.sqrt(norm))[0:1, 0:1]
    last = ring - 2

    def finish(d):
        for u in range(2):
            ring_copy(last, d, u).wait_recv()
        at = part_rows(pos, d)
        dprobs = recv[d, last, 0] + part[0, at]
        logits = (recv[d, last, 1] + part[1, at]) * scale
        top = jnp.max(logits, axis=-1, keepdims=True)
        expo = jnp.exp(logits - top)
        probs = expo / jnp.sum(expo, axis=-1, keepdims=True)
        mean = jnp.sum(probs * dprobs, axis=-1, keepdims=True)
        return probs.astype(BF16), (probs * (dprobs - mean) * scale).astype(BF16)

    grow = rows // gsub

    def pd_rows(chunk, g):
        return pl.ds(pl.multiple_of(chunk * rows + g * grow, 16), grow)

    def chunk_from(s, d):
        return (pos + ring - s) % ring if d == 0 else (pos + s) % ring

    def spread_copy(s, d, g):
        ref = pd.at[pd_rows(chunk_from(s, d), g)]
        return pltpu.make_async_remote_copy(
            src_ref=ref, dst_ref=ref,
            send_sem=g_send.at[d, s, g], recv_sem=g_recv.at[d, s, g],
            device_id=(me, right if d == 0 else left), device_id_type=MESH,
        )

    def keep_copy(s, d, g):
        at = pd_rows(chunk_from(s, d), g)
        return pltpu.make_async_copy(pd.at[at], pd_out.at[at], g_store.at[d, s, g])

    def sends(s, d, g):
        if s < lines - 1:
            return True
        return s == lines - 1 and d == g

    if gsub == 2:
        for d in range(2):
            probs, dlog = finish(d)
            pd[pd_rows(pos, d), 0:cols] = probs
            pd[pd_rows(pos, d), cols:2 * cols] = dlog
            for e in range(2):
                if sends(0, e, d):
                    spread_copy(0, e, d).start()
            keep_copy(0, 0, d).start()
    else:
        a, b = finish(0), finish(1)
        pd[pd_rows(pos, 0), 0:cols] = jnp.concatenate([a[0], b[0]], axis=0)
        pd[pd_rows(pos, 0), cols:2 * cols] = jnp.concatenate([a[1], b[1]], axis=0)
        for e in range(2):
            if sends(0, e, 0):
                spread_copy(0, e, 0).start()
        keep_copy(0, 0, 0).start()

    kept = [(0, 0, g) for g in range(gsub)]
    for s in range(lines):
        for g in range(gsub):
            for e in range(2):
                if sends(s, e, g):
                    spread_copy(s, e, g).wait_recv()
                    if sends(s + 1, e, g):
                        spread_copy(s + 1, e, g).start()
                    keep_copy(s + 1, e, g).start()
                    kept.append((s + 1, e, g))

    for t in range(2):
        for m, b in pairs:
            weight_copy(t, m, b).wait_send()
    for s in range(ring - 1):
        for u in range(2):
            for d in range(2):
                ring_copy(s, d, u).wait_send()
    for s in range(lines):
        for g in range(gsub):
            for e in range(2):
                if sends(s, e, g):
                    spread_copy(s, e, g).wait_send()
    for c in stores:
        c.wait()
    for s, e, g in kept:
        keep_copy(s, e, g).wait()


def output_kernel(qc, kc, vc, gc, wg, pd, depths, att, grad, stacked):
    slots, cols, inner = att.shape[1:]
    hd = inner // HEADS
    depth = depths[lax.axis_index("dp")]
    first = lax.axis_index("row") * slots
    live = [live_of(depth, first + r) for r in range(slots)]
    for h in range(0, HEADS, 2):
        got = []
        for k in range(2):
            n = h + k
            at = slice(n * cols, (n + 1) * cols)
            probs = pd[at, 0:cols]
            dlog = pd[at, cols:2 * cols]
            got.append((
                nn(probs, vc[n]),
                nn(dlog, kc[n]).astype(BF16),
                tn(dlog, qc[n]).astype(BF16),
                tn(probs, gc[n]).astype(BF16),
            ))
        lanes = slice(h * hd, (h + 2) * hd)
        for r in range(slots):
            cut = slice(r * hd, (r + 1) * hd)
            both = [jnp.concatenate([g[i][:, cut] for g in got], axis=1) for i in range(4)]
            att[0, r, :, lanes] = (both[0] * live[r]).astype(BF16)
            for i in range(3):
                stacked[r, :, i * inner + h * hd:i * inner + (h + 2) * hd] = both[i + 1]
    for r in range(slots):
        total = nt(stacked[r], wg[...])
        grad[0, r] = (total * live[r]).astype(BF16)


def local(dp, ring, features, cotangent, projections, depths):
    _, slots, cols, width = features.shape
    inner = projections.shape[2]
    wide = slots * (inner // HEADS)
    rows = HEADS * cols // ring
    gsub = 2 if rows % 32 == 0 else 1
    _, pairs = gather_copies(dp)
    vmem = pl.BlockSpec(memory_space=pltpu.VMEM)
    hbm = pl.BlockSpec(memory_space=pltpu.HBM)
    anyspace = pl.BlockSpec(memory_space=pl.ANY)
    smem = pl.BlockSpec(memory_space=pltpu.SMEM)
    byhead = jax.ShapeDtypeStruct((HEADS, cols, wide), BF16)
    weights = (width, 3 * inner)
    pairshape = (HEADS * cols, 2 * cols)
    lines = ring // 2
    dma = pltpu.SemaphoreType.DMA
    *shaped, wg, pd = pl.pallas_call(
        functools.partial(tied_kernel, dp, ring, gsub),
        out_shape=(
            byhead, byhead, byhead, byhead,
            jax.ShapeDtypeStruct(weights, BF16),
            jax.ShapeDtypeStruct(pairshape, BF16),
        ),
        in_specs=[hbm, hbm, hbm, smem],
        out_specs=[anyspace] * 6,
        scratch_shapes=[
            pltpu.VMEM((slots, cols, width), BF16),
            pltpu.VMEM((slots, cols, inner), BF16),
            pltpu.VMEM(weights, BF16),
            *[pltpu.VMEM((HEADS, cols, wide), BF16)] * 4,
            pltpu.VMEM((2, HEADS * cols, cols), F32),
            pltpu.VMEM((2, ring - 1, 2, rows // 2, cols), F32),
            pltpu.VMEM(pairshape, BF16),
            dma((5,)),
            dma((5,)),
            dma((2, len(pairs))),
            dma((2, len(pairs))),
            dma((2, ring - 1, 2)),
            dma((2, ring - 1, 2)),
            dma((2, lines, gsub)),
            dma((2, lines, gsub)),
            dma((2, lines + 1, gsub)),
        ],
        compiler_params=pltpu.CompilerParams(
            collective_id=0, has_side_effects=True, vmem_limit_bytes=40 * 2**20
        ),
    )(features, cotangent, projections, depths)
    return pl.pallas_call(
        output_kernel,
        out_shape=(
            jax.ShapeDtypeStruct((1, slots, cols, inner), BF16),
            jax.ShapeDtypeStruct((1, slots, cols, width), BF16),
        ),
        in_specs=[vmem] * 6 + [smem],
        out_specs=[vmem] * 2,
        scratch_shapes=[pltpu.VMEM((slots, cols, 3 * inner), BF16)],
        compiler_params=pltpu.CompilerParams(vmem_limit_bytes=40 * 2**20),
    )(*shaped, wg, pd, depths)


def solution(mesh):
    return jax.shard_map(
        functools.partial(local, mesh.shape["dp"], mesh.shape["row"]),
        mesh=mesh,
        in_specs=(P("dp", "row", None, None), P("dp", "row", None, None), P(None, "dp", None), P()),
        out_specs=(P("dp", "row", None, None), P("dp", "row", None, None)),
        check_vma=False,
    )
```

time: 84.6 us -> 83.3 us (0.985)
  Pallas kernels: 79.5 us -> 78.2 us
    pallas_call x1, Pallas kernels: 6.17 us -> 4.85 us  [local(): pl.pallas_call(output_kernel, out_shape=(jax.ShapeDtypeStruct((1, slots,...]
where the time goes in v2:
time: 83.3 us; the launch traced here: 83.1 us
  Pallas kernels  78.2 us (94%)
  local copies, waits for them, and re-layouts  4.2 us (5%)
    pallas_call x1, Pallas kernels, local(): pl.pallas_call(functools.partial(tied_kernel, dp, ring, gsub), out_shape=...  73.4 us
    pallas_call x1, Pallas kernels, local(): pl.pallas_call(output_kernel, out_shape=(jax.ShapeDtypeStruct((1, slots,...  4.85 us
    unnamed x8, local copies, waits for them, and re-layouts  4.2 us

profile of v2, /device:TPU:0, one launch (start us, length us, event | category | flops | bytes accessed | tf_op | source)
XLA Modules:
  0.0 83.1 jit_solution(12902306353841159313)
XLA Ops:
  0.6 0.0 copy-start
  0.6 1.4 %copy-done = bf16[1,4,256,768]{3,2,1,0:T(8,128)(2,1)S(1)} copy-done((bf16[1,4,256,768]{3,2,1,0:T(8,128)(2,1)S(1)}, bf16[1,4,256,768]{3,2,1,0:T(8,128)(2,1)}, u32[]{:S(2)}) %copy-start) | copy-done | bytes 1572888
  2.0 0.0 copy-start.1
  2.0 1.1 %copy-done.1 = bf16[1,4,256,384]{3,2,1,0:T(8,128)(2,1)S(1)} copy-done((bf16[1,4,256,384]{3,2,1,0:T(8,128)(2,1)S(1)}, bf16[1,4,256,384]{3,2,1,0:T(8,128)(2,1)}, u32[]{:S(2)}) %copy-start.1) | copy-done | bytes 786456
  3.2 0.0 copy-start.2
  3.2 1.0 %copy-done.2 = bf16[3,192,384]{2,1,0:T(8,128)(2,1)S(1)} copy-done((bf16[3,192,384]{2,1,0:T(8,128)(2,1)S(1)}, bf16[3,192,384]{2,1,0:T(8,128)(2,1)}, u32[]{:S(2)}) %copy-start.2) | copy-done | bytes 442392
  4.2 0.0 copy-start.3
  4.2 0.7 copy-done.3
  4.8 73.4 %shard_map.59 = (bf16[6,256,256]{2,1,0:T(8,128)(2,1)S(1)}, bf16[6,256,256]{2,1,0:T(8,128)(2,1)S(1)}, bf16[6,256,256]{2,1,0:T(8,128)(2,1)S(1)}, bf16[6,256,256]{2...) custom-call(bf16[1,4,256,768]{3,2,1,0:T(8,128)(2,1)S(1)} %copy-done, ...), custom_call_target="tpu_custom_call" | custom-call | tf_op jit(solution)/shard_map/pallas_call | solution.py:347
  78.2 4.9 %shard_map.60 = (bf16[1,4,256,384]{3,2,1,0:T(8,128)(2,1)}, bf16[1,4,256,768]{3,2,1,0:T(8,128)(2,1)}) custom-call(bf16[6,256,256]{2,1,0:T(8,128)(2,1)S(1)} %get-tuple-element.8.qc, bf16[6,256,256]{2,1,0:T(8,128)(2,1)S(1)} %get-tuple-element.9.kc, bf16[6,256,256]{2,1,0:T(8,128)(2,1)S(1)} %get-tuple-element.10.vc, ...), custom_call_target="tpu_custom_call" | custom-call | tf_op jit(solution)/shard_map/pallas_call | solution.py:378
Async XLA Ops:
  0.6 1.4 %copy-start = (bf16[1,4,256,768]{3,2,1,0:T(8,128)(2,1)S(1)}, bf16[1,4,256,768]{3,2,1,0:T(8,128)(2,1)}, u32[]{:S(2)}) copy-start(bf16[1,4,256,768]{3,2,1,0:T(8,128)(2,1)} %feats_hbm.1) | copy-start | bytes 4718596
  2.0 1.1 %copy-start.1 = (bf16[1,4,256,384]{3,2,1,0:T(8,128)(2,1)S(1)}, bf16[1,4,256,384]{3,2,1,0:T(8,128)(2,1)}, u32[]{:S(2)}) copy-start(bf16[1,4,256,384]{3,2,1,0:T(8,128)(2,1)} %cot_hbm.1) | copy-start | bytes 2359300
  3.2 1.0 %copy-start.2 = (bf16[3,192,384]{2,1,0:T(8,128)(2,1)S(1)}, bf16[3,192,384]{2,1,0:T(8,128)(2,1)}, u32[]{:S(2)}) copy-start(bf16[3,192,384]{2,1,0:T(8,128)(2,1)} %proj_hbm.1) | copy-start | bytes 1327108
  4.2 0.7 copy-start.3

commit v3 on v2

--- a/solution.py
+++ b/solution.py
@@ -59,9 +59,9 @@
 def tied_kernel(
     dp, ring, gsub,
     feats_hbm, cot_hbm, proj_hbm, depths,
-    qc_out, kc_out, vc_out, gc_out, wg_out, pd_out,
-    feats, cot, wg, qc, kc, vc, gc, part, recv, pd,
-    load_sem, store_sem, w_send, w_recv, r_send, r_recv, g_send, g_recv, g_store,
+    att_out, stacked_out, wg_out,
+    feats, cot, wg, qc, kc, vc, gc, part, recv, pd, made, att, stacked,
+    load_sem, store_sem, w_send, w_recv, r_send, r_recv, g_send, g_recv,
 ):
     me = lax.axis_index("dp")
     row = lax.axis_index("row")
@@ -196,14 +196,8 @@
     for d in range(2):
         ring_copy(0, d, 1).start()
 
-    stores = [
-        pltpu.make_async_copy(s, d, store_sem.at[i])
-        for i, (s, d) in enumerate(
-            ((qc, qc_out), (kc, kc_out), (vc, vc_out), (gc, gc_out), (wg, wg_out))
-        )
-    ]
-    for c in stores:
-        c.start()
+    stores = [pltpu.make_async_copy(wg, wg_out, store_sem.at[0])]
+    stores[0].start()
     for s in range(ring - 2):
         if s + 2 < ring - 2:
             hop(s + 2, 0)
@@ -241,10 +235,6 @@
             device_id=(me, right if d == 0 else left), device_id_type=MESH,
         )
 
-    def keep_copy(s, d, g):
-        at = pd_rows(chunk_from(s, d), g)
-        return pltpu.make_async_copy(pd.at[at], pd_out.at[at], g_store.at[d, s, g])
-
     def sends(s, d, g):
         if s < lines - 1:
             return True
@@ -258,7 +248,6 @@
             for e in range(2):
                 if sends(0, e, d):
                     spread_copy(0, e, d).start()
-            keep_copy(0, 0, d).start()
     else:
         a, b = finish(0), finish(1)
         pd[pd_rows(pos, 0), 0:cols] = jnp.concatenate([a[0], b[0]], axis=0)
@@ -266,18 +255,50 @@
         for e in range(2):
             if sends(0, e, 0):
                 spread_copy(0, e, 0).start()
-        keep_copy(0, 0, 0).start()
-
-    kept = [(0, 0, g) for g in range(gsub)]
-    for s in range(lines):
+
+    def arrive(s):
         for g in range(gsub):
             for e in range(2):
                 if sends(s, e, g):
                     spread_copy(s, e, g).wait_recv()
                     if sends(s + 1, e, g):
                         spread_copy(s + 1, e, g).start()
-                    keep_copy(s + 1, e, g).start()
-                    kept.append((s + 1, e, g))
+
+    def head(h):
+        at = pl.ds(pl.multiple_of(h * cols, cols), cols)
+        probs = pd[at, 0:cols]
+        dlog = pd[at, cols:2 * cols]
+        made[0, h] = nn(probs, vc[h]).astype(BF16)
+        made[1, h] = nn(dlog, kc[h]).astype(BF16)
+        made[2, h] = tn(dlog, qc[h]).astype(BF16)
+        made[3, h] = tn(probs, gc[h]).astype(BF16)
+
+    for s in range(lines - 1):
+        arrive(s)
+    far = (pos + lines) % ring
+    after = (far * rows + rows - 1) // cols + 1
+    for k in range(HEADS - 2):
+        head((after + k) % HEADS)
+    arrive(lines - 1)
+    for k in range(HEADS - 2, HEADS):
+        head((after + k) % HEADS)
+
+    for r in range(slots):
+        cut = slice(r * hd, (r + 1) * hd)
+        live = live_of(depth, first + r)
+        for h in range(0, HEADS, 2):
+            both = [
+                jnp.concatenate([made[i, h, :, cut], made[i, h + 1, :, cut]], axis=1)
+                for i in range(4)
+            ]
+            att[r, :, h * hd:(h + 2) * hd] = (both[0].astype(F32) * live).astype(BF16)
+            for i in range(3):
+                lanes = slice(i * inner + h * hd, i * inner + (h + 2) * hd)
+                stacked[r, :, lanes] = both[i + 1]
+        for i, (src, dst) in enumerate(((att, att_out), (stacked, stacked_out))):
+            c = pltpu.make_async_copy(src.at[r], dst.at[r], store_sem.at[1 + 2 * r + i])
+            c.start()
+            stores.append(c)
 
     for t in range(2):
         for m, b in pairs:
@@ -293,39 +314,14 @@
                     spread_copy(s, e, g).wait_send()
     for c in stores:
         c.wait()
-    for s, e, g in kept:
-        keep_copy(s, e, g).wait()
-
-
-def output_kernel(qc, kc, vc, gc, wg, pd, depths, att, grad, stacked):
-    slots, cols, inner = att.shape[1:]
-    hd = inner // HEADS
+
+
+def output_kernel(att_in, stacked, wg, depths, att, grad):
+    slots = pl.num_programs(0)
     depth = depths[lax.axis_index("dp")]
-    first = lax.axis_index("row") * slots
-    live = [live_of(depth, first + r) for r in range(slots)]
-    for h in range(0, HEADS, 2):
-        got = []
-        for k in range(2):
-            n = h + k
-            at = slice(n * cols, (n + 1) * cols)
-            probs = pd[at, 0:cols]
-            dlog = pd[at, cols:2 * cols]
-            got.append((
-                nn(probs, vc[n]),
-                nn(dlog, kc[n]).astype(BF16),
-                tn(dlog, qc[n]).astype(BF16),
-                tn(probs, gc[n]).astype(BF16),
-            ))
-        lanes = slice(h * hd, (h + 2) * hd)
-        for r in range(slots):
-            cut = slice(r * hd, (r + 1) * hd)
-            both = [jnp.concatenate([g[i][:, cut] for g in got], axis=1) for i in range(4)]
-            att[0, r, :, lanes] = (both[0] * live[r]).astype(BF16)
-            for i in range(3):
-                stacked[r, :, i * inner + h * hd:i * inner + (h + 2) * hd] = both[i + 1]
-    for r in range(slots):
-        total = nt(stacked[r], wg[...])
-        grad[0, r] = (total * live[r]).astype(BF16)
+    slot = lax.axis_index("row") * slots + pl.program_id(0)
+    att[0, 0] = att_in[0]
+    grad[0, 0] = (nt(stacked[0], wg[...]) * live_of(depth, slot)).astype(BF16)
 
 
 def local(dp, ring, features, cotangent, projections, depths):
@@ -335,24 +331,22 @@
     rows = HEADS * cols // ring
     gsub = 2 if rows % 32 == 0 else 1
     _, pairs = gather_copies(dp)
-    vmem = pl.BlockSpec(memory_space=pltpu.VMEM)
     hbm = pl.BlockSpec(memory_space=pltpu.HBM)
     anyspace = pl.BlockSpec(memory_space=pl.ANY)
     smem = pl.BlockSpec(memory_space=pltpu.SMEM)
-    byhead = jax.ShapeDtypeStruct((HEADS, cols, wide), BF16)
     weights = (width, 3 * inner)
     pairshape = (HEADS * cols, 2 * cols)
     lines = ring // 2
     dma = pltpu.SemaphoreType.DMA
-    *shaped, wg, pd = pl.pallas_call(
+    att, stacked, wg = pl.pallas_call(
         functools.partial(tied_kernel, dp, ring, gsub),
         out_shape=(
-            byhead, byhead, byhead, byhead,
+            jax.ShapeDtypeStruct((slots, cols, inner), BF16),
+            jax.ShapeDtypeStruct((slots, cols, 3 * inner), BF16),
             jax.ShapeDtypeStruct(weights, BF16),
-            jax.ShapeDtypeStruct(pairshape, BF16),
         ),
         in_specs=[hbm, hbm, hbm, smem],
-        out_specs=[anyspace] * 6,
+        out_specs=[anyspace] * 3,
         scratch_shapes=[
             pltpu.VMEM((slots, cols, width), BF16),
             pltpu.VMEM((slots, cols, inner), BF16),
@@ -361,31 +355,41 @@
             pltpu.VMEM((2, HEADS * cols, cols), F32),
             pltpu.VMEM((2, ring - 1, 2, rows // 2, cols), F32),
             pltpu.VMEM(pairshape, BF16),
+            pltpu.VMEM((4, HEADS, cols, wide), BF16),
+            pltpu.VMEM((slots, cols, inner), BF16),
+            pltpu.VMEM((slots, cols, 3 * inner), BF16),
             dma((5,)),
-            dma((5,)),
+            dma((1 + 2 * slots,)),
             dma((2, len(pairs))),
             dma((2, len(pairs))),
             dma((2, ring - 1, 2)),
             dma((2, ring - 1, 2)),
             dma((2, lines, gsub)),
             dma((2, lines, gsub)),
-            dma((2, lines + 1, gsub)),
         ],
         compiler_params=pltpu.CompilerParams(
-            collective_id=0, has_side_effects=True, vmem_limit_bytes=40 * 2**20
+            collective_id=0, has_side_effects=True, vmem_limit_bytes=58 * 2**20
         ),
     )(features, cotangent, projections, depths)
     return pl.pallas_call(
         output_kernel,
+        grid=(slots,),
         out_shape=(
             jax.ShapeDtypeStruct((1, slots, cols, inner), BF16),
             jax.ShapeDtypeStruct((1, slots, cols, width), BF16),
         ),
-        in_specs=[vmem] * 6 + [smem],
-        out_specs=[vmem] * 2,
-        scratch_shapes=[pltpu.VMEM((slots, cols, 3 * inner), BF16)],
-        compiler_params=pltpu.CompilerParams(vmem_limit_bytes=40 * 2**20),
-    )(*shaped, wg, pd, depths)
+        in_specs=[
+            pl.BlockSpec((1, cols, inner), lambda r: (r, 0, 0)),
+            pl.BlockSpec((1, cols, 3 * inner), lambda r: (r, 0, 0)),
+            pl.BlockSpec(weights, lambda r: (0, 0)),
+            smem,
+        ],
+        out_specs=[
+            pl.BlockSpec((1, 1, cols, inner), lambda r: (0, r, 0, 0)),
+            pl.BlockSpec((1, 1, cols, width), lambda r: (0, r, 0, 0)),
+        ],
+        compiler_params=pltpu.CompilerParams(vmem_limit_bytes=60 * 2**20),
+    )(att, stacked, wg, depths)
 
 
 def solution(mesh):

time: 83.3 us -> 82.5 us (level)
  local copies, waits for them, and re-layouts: 4.2 us -> 0 us
  Pallas kernels: 78.2 us -> 81.7 us
    unnamed x8 -> x0, local copies, waits for them, and re-layouts: 4.2 us -> none
    pallas_call x1, Pallas kernels: 73.4 us -> 75.6 us  [local(): pl.pallas_call(functools.partial(tied_kernel, dp, ring, gsub), out_shape=...]
    pallas_call x1, Pallas kernels: 4.85 us -> 6.11 us  [local(): pl.pallas_call(output_kernel, grid=(slots,), out_shape=(jax.ShapeDtypeStr...]
where the time goes in v3:
time: 82.5 us; the launch traced here: 82.3 us
  Pallas kernels  81.7 us (99%)
    pallas_call x1, Pallas kernels, local(): pl.pallas_call(functools.partial(tied_kernel, dp, ring, gsub), out_shape=...  75.6 us
    pallas_call x1, Pallas kernels, local(): pl.pallas_call(output_kernel, grid=(slots,), out_shape=(jax.ShapeDtypeStr...  6.11 us

profile of v3, /device:TPU:0, one launch (start us, length us, event | category | flops | bytes accessed | tf_op | source)
XLA Modules:
  0.0 82.3 jit_solution(4364371241489318478)
XLA Ops:
  0.6 75.6 %shard_map.59 = (bf16[4,256,384]{2,1,0:T(8,128)(2,1)}, bf16[4,256,1152]{2,1,0:T(8,128)(2,1)}, bf16[768,1152]{1,0:T(8,128)(2,1)}) custom-call(bf16[1,4,256,768]{3,2,1,0:T(8,128)(2,1)} %feats_hbm.1, bf16[1,4,256,384]{3,2,1,0:T(8,128)(2,1)} %cot_hbm.1, bf16[3,192,384]{2,1,0:T(8,128)(2,1)} %proj_hbm.1, s32[4]{0:T(128)} %depths.3), custom_call_target="tpu_custom_call" | custom-call | tf_op jit(solution)/shard_map/pallas_call | solution.py:341
  76.2 6.1 %shard_map.60 = (bf16[1,4,256,384]{3,2,1,0:T(8,128)(2,1)}, bf16[1,4,256,768]{3,2,1,0:T(8,128)(2,1)}) custom-call(bf16[4,256,384]{2,1,0:T(8,128)(2,1)} %get-tuple-element.5.att_in, bf16[4,256,1152]{2,1,0:T(8,128)(2,1)} %get-tuple-element.6.stacked, bf16[768,1152]{1,0:T(8,128)(2,1)} %get-tuple-element.7.wg, s32[4]{0:T(128)} %depths.3), custom_call_target="tpu_custom_call" | custom-call | tf_op jit(solution)/shard_map/pallas_call | solution.py:374

commit v4 on v3

--- a/solution.py
+++ b/solution.py
@@ -153,7 +153,8 @@
     loads[4].wait()
     for r in range(0, slots, 2):
         by_head(gc, [cot[r + k].astype(F32) * l for k, l in enumerate(live_at(r))], r)
-        by_head(vc, [nn(feats[r + k], wg[:, groups[0]]) for k in range(2)], r)
+        val = nn(feats[r:r + 2].reshape(2 * cols, -1), wg[:, groups[0]])
+        by_head(vc, [val[:cols], val[cols:]], r)
     for h in range(HEADS):
         part[0, h * cols:(h + 1) * cols, :] = nt(gc[h], vc[h])
 
@@ -186,7 +187,8 @@
     for b in bits[1:]:
         weights_from(1, b)
     for r in range(0, slots, 2):
-        both = [nn(feats[r + k], wg[:, groups[1]]) for k in range(2)]
+        both = nn(feats[r:r + 2].reshape(2 * cols, -1), wg[:, groups[1]])
+        both = [both[:cols], both[cols:]]
         by_head(qc, [v[:, :inner] * l for v, l in zip(both, live_at(r))], r)
         by_head(kc, [v[:, inner:] for v in both], r)
         if r == 0:
@@ -317,11 +319,14 @@
 
 
 def output_kernel(att_in, stacked, wg, depths, att, grad):
-    slots = pl.num_programs(0)
+    slots, cols, wide = stacked.shape
     depth = depths[lax.axis_index("dp")]
-    slot = lax.axis_index("row") * slots + pl.program_id(0)
-    att[0, 0] = att_in[0]
-    grad[0, 0] = (nt(stacked[0], wg[...]) * live_of(depth, slot)).astype(BF16)
+    first = lax.axis_index("row") * slots
+    att[0] = att_in[...]
+    total = nt(stacked[...].reshape(slots * cols, wide), wg[...])
+    for r in range(slots):
+        part = total[r * cols:(r + 1) * cols]
+        grad[0, r] = (part * live_of(depth, first + r)).astype(BF16)
 
 
 def local(dp, ring, features, cotangent, projections, depths):
@@ -373,20 +378,20 @@
     )(features, cotangent, projections, depths)
     return pl.pallas_call(
         output_kernel,
-        grid=(slots,),
+        grid=(3,),
         out_shape=(
             jax.ShapeDtypeStruct((1, slots, cols, inner), BF16),
             jax.ShapeDtypeStruct((1, slots, cols, width), BF16),
         ),
         in_specs=[
-            pl.BlockSpec((1, cols, inner), lambda r: (r, 0, 0)),
-            pl.BlockSpec((1, cols, 3 * inner), lambda r: (r, 0, 0)),
-            pl.BlockSpec(weights, lambda r: (0, 0)),
+            pl.BlockSpec((slots, cols, inner // 3), lambda n: (0, 0, n)),
+            pl.BlockSpec((slots, cols, 3 * inner), lambda n: (0, 0, 0)),
+            pl.BlockSpec((width // 3, 3 * inner), lambda n: (n, 0)),
             smem,
         ],
         out_specs=[
-            pl.BlockSpec((1, 1, cols, inner), lambda r: (0, r, 0, 0)),
-            pl.BlockSpec((1, 1, cols, width), lambda r: (0, r, 0, 0)),
+            pl.BlockSpec((1, slots, cols, inner // 3), lambda n: (0, 0, 0, n)),
+            pl.BlockSpec((1, slots, cols, width // 3), lambda n: (0, 0, 0, n)),
         ],
         compiler_params=pltpu.CompilerParams(vmem_limit_bytes=60 * 2**20),
     )(att, stacked, wg, depths)

time: 82.5 us -> 82.1 us (level)
  no operation moved by 1% of the time
where the time goes in v4:
time: 82.1 us; the launch traced here: 82 us
  Pallas kernels  81.3 us (99%)
    pallas_call x1, Pallas kernels, local(): pl.pallas_call(functools.partial(tied_kernel, dp, ring, gsub), out_shape=...  75.4 us
    pallas_call x1, Pallas kernels, local(): pl.pallas_call(output_kernel, grid=(3,), out_shape=(jax.ShapeDtypeStruct(...  5.94 us

profile of v4, /device:TPU:0, one launch (start us, length us, event | category | flops | bytes accessed | tf_op | source)
XLA Modules:
  0.0 82.0 jit_solution(15559231772894372070)
XLA Ops:
  0.6 75.4 %shard_map.59 = (bf16[4,256,384]{2,1,0:T(8,128)(2,1)}, bf16[4,256,1152]{2,1,0:T(8,128)(2,1)}, bf16[768,1152]{1,0:T(8,128)(2,1)}) custom-call(bf16[1,4,256,768]{3,2,1,0:T(8,128)(2,1)} %feats_hbm.1, bf16[1,4,256,384]{3,2,1,0:T(8,128)(2,1)} %cot_hbm.1, bf16[3,192,384]{2,1,0:T(8,128)(2,1)} %proj_hbm.1, s32[4]{0:T(128)} %depths.3), custom_call_target="tpu_custom_call" | custom-call | tf_op jit(solution)/shard_map/pallas_call | solution.py:346
  76.0 5.9 %shard_map.60 = (bf16[1,4,256,384]{3,2,1,0:T(8,128)(2,1)}, bf16[1,4,256,768]{3,2,1,0:T(8,128)(2,1)}) custom-call(bf16[4,256,384]{2,1,0:T(8,128)(2,1)} %get-tuple-element.5.att_in, bf16[4,256,1152]{2,1,0:T(8,128)(2,1)} %get-tuple-element.6.stacked, bf16[768,1152]{1,0:T(8,128)(2,1)} %get-tuple-element.7.wg, s32[4]{0:T(128)} %depths.3), custom_call_target="tpu_custom_call" | custom-call | tf_op jit(solution)/shard_map/pallas_call | solution.py:379

commit v5 on v4

--- a/solution.py
+++ b/solution.py
@@ -128,6 +128,24 @@
     loads[2].wait()
     for b in bits:
         weight_copy(0, 0, b).start()
+
+    depth = depths[me]
+    first = row * slots
+
+    def by_head(dest, vals, r):
+        vals = [v.astype(BF16) for v in vals]
+        for h in range(HEADS):
+            dest[h, :, r * hd:(r + 2) * hd] = jnp.concatenate(
+                [v[:, h * hd:(h + 1) * hd] for v in vals], axis=1
+            )
+
+    def live_at(r):
+        return [live_of(depth, first + r + k) for k in range(2)]
+
+    loads[4].wait()
+    for r in range(0, slots, 2):
+        by_head(gc, [cot[r + k].astype(F32) * l for k, l in enumerate(live_at(r))], r)
+    loads[3].wait()
     weights_from(0, bits[0])
     loads[0].wait()
     loads[1].wait()
@@ -135,24 +153,7 @@
         weight_copy(1, 0, b).start()
     for b in bits[1:]:
         weights_from(0, b)
-
-    depth = depths[me]
-    first = row * slots
-
-    def by_head(dest, vals, r):
-        vals = [v.astype(BF16) for v in vals]
-        for h in range(HEADS):
-            dest[h, :, r * hd:(r + 2) * hd] = jnp.concatenate(
-                [v[:, h * hd:(h + 1) * hd] for v in vals], axis=1
-            )
-
-    def live_at(r):
-        return [live_of(depth, first + r + k) for k in range(2)]
-
-    loads[3].wait()
-    loads[4].wait()
     for r in range(0, slots, 2):
-        by_head(gc, [cot[r + k].astype(F32) * l for k, l in enumerate(live_at(r))], r)
         val = nn(feats[r:r + 2].reshape(2 * cols, -1), wg[:, groups[0]])
         by_head(vc, [val[:cols], val[cols:]], r)
     for h in range(HEADS):

time: 82.1 us -> 81.9 us (level)
  no operation moved by 1% of the time
where the time goes in v5:
time: 81.9 us; the launch traced here: 81.8 us
  Pallas kernels  81.1 us (99%)
    pallas_call x1, Pallas kernels, local(): pl.pallas_call(functools.partial(tied_kernel, dp, ring, gsub), out_shape=...  75.2 us
    pallas_call x1, Pallas kernels, local(): pl.pallas_call(output_kernel, grid=(3,), out_shape=(jax.ShapeDtypeStruct(...  5.95 us

profile of v5, /device:TPU:0, one launch (start us, length us, event | category | flops | bytes accessed | tf_op | source)
XLA Modules:
  0.0 81.8 jit_solution(11650064933869812070)
XLA Ops:
  0.6 75.2 %shard_map.59 = (bf16[4,256,384]{2,1,0:T(8,128)(2,1)}, bf16[4,256,1152]{2,1,0:T(8,128)(2,1)}, bf16[768,1152]{1,0:T(8,128)(2,1)}) custom-call(bf16[1,4,256,768]{3,2,1,0:T(8,128)(2,1)} %feats_hbm.1, bf16[1,4,256,384]{3,2,1,0:T(8,128)(2,1)} %cot_hbm.1, bf16[3,192,384]{2,1,0:T(8,128)(2,1)} %proj_hbm.1, s32[4]{0:T(128)} %depths.3), custom_call_target="tpu_custom_call" | custom-call | tf_op jit(solution)/shard_map/pallas_call | solution.py:347
  75.8 5.9 %shard_map.60 = (bf16[1,4,256,384]{3,2,1,0:T(8,128)(2,1)}, bf16[1,4,256,768]{3,2,1,0:T(8,128)(2,1)}) custom-call(bf16[4,256,384]{2,1,0:T(8,128)(2,1)} %get-tuple-element.5.att_in, bf16[4,256,1152]{2,1,0:T(8,128)(2,1)} %get-tuple-element.6.stacked, bf16[768,1152]{1,0:T(8,128)(2,1)} %get-tuple-element.7.wg, s32[4]{0:T(128)} %depths.3), custom_call_target="tpu_custom_call" | custom-call | tf_op jit(solution)/shard_map/pallas_call | solution.py:380
